TPU v7x, 32 devices: a whole 2x2x4 slice. The times are simulated.
32 devices in a mesh: groups: 2 (over y), dp: 4 (over x, core), tensor: 4 (over z).
Axes of the slice: x: 2, y: 2, z: 4, core: 2. Of those that a mesh axis runs over, the one named last changes fastest.
Arguments:
- x_stream: bfloat16 [1024, 2048], P(('groups', 'dp'), 'tensor'), parts along dimension 0, may hold values from -24 to 24
- bc_stream: bfloat16 [1024, 1024], P(('groups', 'dp'), 'tensor'), parts along dimension 0, may hold values from -5 to 5
- gate_stream: bfloat16 [1024, 2048], P(('groups', 'dp'), 'tensor'), parts along dimension 0, may hold values from -5 to 5
- dt_stream: bfloat16 [1024, 32], P(('groups', 'dp'), 'tensor'), parts along dimension 0, may hold values from -4 to 4
- conv_x_state: bfloat16 [32, 3, 2048], P(('groups', 'dp'), None, 'tensor'), parts along dimension 0, may hold values from -5 to 5
- conv_bc_state: bfloat16 [32, 3, 1024], P(('groups', 'dp'), None, 'tensor'), parts along dimension 0, may hold values from -5 to 5
- ssm_state: bfloat16 [32, 32, 64, 256], P(('groups', 'dp'), 'tensor'), parts along dimension 0, may hold values from -5 to 5
- conv_x_weight: bfloat16 [4, 2048], P(None, 'tensor'), may hold values from -3 to 3
- conv_bc_weight: bfloat16 [4, 1024], P(None, 'tensor'), may hold values from -3 to 3
- dt_bias: float32 [32], P('tensor'), may hold values from -3 to 0
- decay_rate: float32 [32], P('tensor'), may hold values from 0.01 to 0.5
- skip_gain: float32 [32], P('tensor'), may hold values from 0.5 to 2
- norm_gain: float32 [2048], P('tensor'), may hold values from 0.25 to 1.75
- parents: int32 [32, 32], P(('groups', 'dp')), parts along dimension 0, may hold values from -1 to 30, as said below
- accepted: int32 [32], P(('groups', 'dp')), parts along dimension 0, may hold values from 0 to 31
- destination: int32 [32], P('groups'), parts along dimension 0, may hold values from -1 to 3, as said below
Outputs:
- y_out: bfloat16 [1024, 2048], P(('groups', 'dp'), 'tensor'), parts along dimension 0
- new_ssm_state: bfloat16 [48, 32, 64, 256], P(('groups', 'dp'), 'tensor'), parts along dimension 0
- new_conv_x: bfloat16 [48, 3, 2048], P(('groups', 'dp'), None, 'tensor'), parts along dimension 0
- new_conv_bc: bfloat16 [48, 3, 1024], P(('groups', 'dp'), None, 'tensor'), parts along dimension 0
There are 2 independent parts, one for each index of `groups`. A program takes and returns all parts, laid end to end along the dimension named above; an argument that names none is the same for every part. Nothing has to cross between parts.
Inputs may be any that keep to these rules, and one draw needn't show every extreme that they name: `parents`: node 0 is the root with parent -1; every other node's parent is an earlier node. Exactly 2 of the 4 requests of each data index have a destination other than -1; no data index is the destination of more than 4 requests, and some data index is the destination of exactly 4.
All inputs are finite; a program needn't handle non-finite values.
Results may differ from a plain program's by a relative error of at most 0.006.
Values may be sent and summed in bfloat16 or wider, within the bound.
A program may use at most 64 MiB of HBM per device.

v0:
```python
import jax
import jax.numpy as jnp
from jax import lax
from jax.sharding import PartitionSpec as P

P_SIZE = 64
N = 256
NODES = 32
MOVE = 2
IN_CAP = 4
KEEP = 6


def from_partner(x, axis, distance):
    return lax.ppermute(x, axis, [(i, i ^ 1 << distance) for i in range(lax.axis_size(axis))])


def chain_product(left, right):
    return jnp.einsum("rij,rjk->rik", left, right, precision=lax.Precision.HIGHEST)


def convolve(values, history, weight, tap_pick):
    combined = jnp.concatenate([values, history], axis=1)
    tapped = jnp.einsum("krij,rjc->kric", tap_pick, combined, preferred_element_type=jnp.float32)
    tapped = lax.optimization_barrier(tapped)
    summed = weight[0].astype(jnp.float32) * tapped[0]
    for k in range(1, 4):
        summed = summed + weight[k].astype(jnp.float32) * tapped[k]
    return jax.nn.silu(summed).astype(jnp.bfloat16)


def latest_taps(values, history, accept_hot, tap_float):
    combined = jnp.concatenate([values, history], axis=1)
    collected = []
    for t in range(3):
        row = jnp.einsum("ri,rij->rj", accept_hot, tap_float[2 - t]).astype(jnp.bfloat16)
        picked = jnp.einsum("rj,rjc->rc", row, combined, preferred_element_type=jnp.float32)
        collected.append(picked.astype(jnp.bfloat16))
    return jnp.stack(collected, axis=1)


def body(
    x_stream,
    bc_stream,
    gate_stream,
    dt_stream,
    conv_x_state,
    conv_bc_state,
    ssm_state,
    conv_x_weight,
    conv_bc_weight,
    dt_bias,
    decay_rate,
    skip_gain,
    norm_gain,
    parents,
    accepted,
    destination,
):
    requests = parents.shape[0]
    heads_here = dt_stream.shape[1]
    node_ids = jnp.arange(NODES)
    parent_hot = (parents[:, :, None] == node_ids[None, None, :]).astype(jnp.float32)
    identity = jnp.broadcast_to(jnp.eye(NODES, dtype=jnp.float32), parent_hot.shape)
    on_path = identity
    stride = parent_hot
    for turn in range((NODES - 1).bit_length()):
        reached_more = lax.optimization_barrier(chain_product(stride, on_path))
        on_path = on_path + reached_more
        stride = chain_product(stride, stride)
    depths = jnp.sum(on_path, axis=2) - 1.0
    hop_float = [identity, parent_hot]
    for k in range(2, 4):
        hop_float.append(chain_product(hop_float[-1], parent_hot))
    tap_float = []
    for k in range(4):
        wanted = 3.0 - jnp.arange(3, dtype=jnp.float32)
        lag_part = ((k - depths)[:, :, None] == wanted[None, None, :]).astype(jnp.float32)
        tap_float.append(jnp.concatenate([hop_float[k], lag_part], axis=2))
    tap_pick = jnp.stack(tap_float).astype(jnp.bfloat16)
    x_rows = x_stream.reshape(requests, NODES, -1)
    bc_rows = bc_stream.reshape(requests, NODES, -1)
    parity = lax.axis_index("tensor") % 2
    own_act = convolve(bc_rows, conv_bc_state, conv_bc_weight, tap_pick)
    other_act = from_partner(own_act, "tensor", 0)
    b_act = jnp.where(parity == 0, own_act, other_act)
    c_act = jnp.where(parity == 0, other_act, own_act)
    x_act = convolve(x_rows, conv_x_state, conv_x_weight, tap_pick)
    step_size = jax.nn.softplus(
        dt_stream.reshape(requests, NODES, heads_here).astype(jnp.float32) + dt_bias
    )
    step_decay = -decay_rate * step_size
    logdecay = jnp.einsum("rij,rjh->rih", on_path, step_decay, precision=lax.Precision.HIGHEST)
    inner = jnp.einsum("rin,rjn->rij", c_act, b_act, preferred_element_type=jnp.float32)
    inside = (on_path > 0.5)[..., None]
    spread = jnp.where(inside, logdecay[:, :, None, :] - logdecay[:, None, :, :], -1e30)
    decay = jnp.where(inside, jnp.exp(spread), 0.0) * step_size[:, None, :, :]
    weights = (inner[..., None] * decay).astype(jnp.bfloat16)
    x_heads = x_act.reshape(requests, NODES, heads_here, P_SIZE)
    tree_part = jnp.einsum("rijh,rjhp->rihp", weights, x_heads, preferred_element_type=jnp.float32)
    held = jnp.einsum("rin,rhpn->rihp", c_act, ssm_state, preferred_element_type=jnp.float32)
    tree_part, held = lax.optimization_barrier((tree_part, held))
    held = held * jnp.exp(logdecay)[..., None]
    mixed = tree_part + held + skip_gain[:, None] * x_heads.astype(jnp.float32)
    gated = mixed * jax.nn.silu(
        gate_stream.reshape(requests, NODES, heads_here, P_SIZE).astype(jnp.float32)
    )
    squares = jnp.sum(gated * gated, axis=(2, 3))
    partner_squares = from_partner(squares, "tensor", 0)
    mean_square = (squares + partner_squares) / (2 * heads_here * P_SIZE)
    normed = (
        gated
        * lax.rsqrt(mean_square + 1e-05)[:, :, None, None]
        * norm_gain.reshape(heads_here, P_SIZE)
    )
    y_out = normed.astype(jnp.bfloat16).reshape(requests * NODES, heads_here * P_SIZE)
    accept_hot = (accepted[:, None] == node_ids[None, :]).astype(jnp.float32)
    accept_row = jnp.einsum("ri,rij->rj", accept_hot, on_path)
    accept_log = jnp.einsum("ri,rih->rh", accept_hot, logdecay, precision=lax.Precision.HIGHEST)
    reached = (accept_row > 0.5)[..., None]
    reach = jnp.where(reached, accept_log[:, None, :] - logdecay, -1e30)
    coef = (jnp.where(reached, jnp.exp(reach), 0.0) * step_size).astype(jnp.bfloat16)
    scaled_x = coef.astype(jnp.float32)[..., None] * x_heads.astype(jnp.float32)
    update = jnp.einsum(
        "rjhp,rjn->rhpn", scaled_x, b_act.astype(jnp.float32), precision=lax.Precision.HIGHEST
    )
    update = lax.optimization_barrier(update)
    fresh = jnp.exp(accept_log)[:, :, None, None] * ssm_state.astype(jnp.float32) + update
    fresh = fresh.astype(jnp.bfloat16)
    fresh_x = latest_taps(x_rows, conv_x_state, accept_hot, tap_float)
    fresh_bc = latest_taps(bc_rows, conv_bc_state, accept_hot, tap_float)
    state_width = heads_here * P_SIZE * N
    x_width = 3 * heads_here * P_SIZE
    record = jnp.concatenate(
        [
            fresh.reshape(requests, -1),
            fresh_x.reshape(requests, -1),
            fresh_bc.reshape(requests, -1),
        ],
        axis=1,
    )
    me_index = lax.axis_index("dp")
    ndevices = lax.axis_size("dp")
    home_dest = lax.dynamic_slice_in_dim(destination, me_index * requests, requests)
    staying = home_dest < 0
    stay_rank = jnp.cumsum(staying.astype(jnp.int32)) - 1
    move_rank = jnp.cumsum((~staying).astype(jnp.int32)) - 1
    stay_pick = (
        staying[None, :] & (stay_rank[None, :] == jnp.arange(requests - MOVE)[:, None])
    ).astype(jnp.bfloat16)
    move_pick = ((~staying)[None, :] & (move_rank[None, :] == jnp.arange(MOVE)[:, None])).astype(
        jnp.bfloat16
    )
    kept = jnp.dot(stay_pick, record, preferred_element_type=jnp.float32).astype(jnp.bfloat16)
    packed = jnp.dot(move_pick, record, preferred_element_type=jnp.float32).astype(jnp.bfloat16)
    grid = destination.reshape(ndevices, requests)
    moving = grid >= 0
    grid_rank = jnp.cumsum(moving.astype(jnp.int32), axis=1) - 1
    mover_hot = moving[:, None, :] & (grid_rank[:, None, :] == jnp.arange(MOVE)[None, :, None])
    mover_dest = jnp.sum(jnp.where(mover_hot, grid[:, None, :], 0), axis=2).reshape(ndevices * MOVE)
    dest_hot = (mover_dest[:, None] == jnp.arange(ndevices)[None, :]).astype(jnp.int32)
    mover_slot = jnp.sum((jnp.cumsum(dest_hot, axis=0) - 1) * dest_hot, axis=1)
    placed = jnp.dot(
        (
            (mover_dest[None, :] == me_index) & (mover_slot[None, :] == jnp.arange(IN_CAP)[:, None])
        ).astype(jnp.bfloat16),
        lax.all_gather(packed, "dp", axis=0, tiled=True),
        preferred_element_type=jnp.float32,
    ).astype(jnp.bfloat16)
    placed = lax.optimization_barrier(placed)
    blocks = jnp.concatenate([kept, placed], axis=0)
    new_ssm_state = blocks[:, :state_width].reshape(KEEP, heads_here, P_SIZE, N)
    new_conv_x = blocks[:, state_width : state_width + x_width].reshape(
        KEEP, 3, heads_here * P_SIZE
    )
    new_conv_bc = blocks[:, state_width + x_width :].reshape(KEEP, 3, -1)
    return (y_out, new_ssm_state, new_conv_x, new_conv_bc)


def solution(mesh):
    placed = (
        P(("groups", "dp"), "tensor"),
        P(("groups", "dp"), "tensor"),
        P(("groups", "dp"), "tensor"),
        P(("groups", "dp"), "tensor"),
        P(("groups", "dp"), None, "tensor"),
        P(("groups", "dp"), None, "tensor"),
        P(("groups", "dp"), "tensor", None, None),
        P(None, "tensor"),
        P(None, "tensor"),
        P("tensor"),
        P("tensor"),
        P("tensor"),
        P("tensor"),
        P(("groups", "dp"), None),
        P(("groups", "dp")),
        P("groups"),
    )
    return jax.shard_map(
        body,
        mesh=mesh,
        in_specs=placed,
        out_specs=(
            P(("groups", "dp"), "tensor"),
            P(("groups", "dp"), "tensor", None, None),
            P(("groups", "dp"), None, "tensor"),
            P(("groups", "dp"), None, "tensor"),
        ),
        check_vma=False,
    )
```

profile of v0, /device:TPU:0, one launch (start us, length us, event | category | flops | bytes accessed | tf_op | source)
XLA Modules:
  0.0 75.2 jit_solution(11827031706455856950)
XLA Ops:
  7.2 0.8 %iota_compare_fusion = pred[4,32,32]{2,1,0:T(32,128)(4,1)S(1)} fusion(s32[4,32]{1,0:T(4,128)} %param.29), kind=kLoop, calls=%fused_computation.65 | loop fusion | flops 4096 | bytes 4608 | tf_op jit(solution)/shard_map/eq | solution.py:63
  8.0 1.0 %fusion.34 = f32[4,32,32]{2,1,0:T(8,128)S(1)} fusion(s32[4,32]{1,0:T(4,128)} %param.29), kind=kOutput, calls=%fused_computation.76 | convolution fusion | flops 266240 | bytes 16896 | tf_op jit(solution)/shard_map/rij,rjk->rik/dot_general | solution.py:19
  9.0 0.9 %convolution_convert_fusion.3 = bf16[4,32,32]{2,1,0:T(8,128)(2,1)S(1)} fusion(f32[4,32,32]{2,1,0:T(8,128)S(1)} %fusion.34, s32[4,32]{1,0:T(4,128)} %param.29), kind=kOutput, calls=%fused_computation.13 | convolution fusion | flops 1581056 | bytes 25088 | tf_op jit(solution)/shard_map/rij,rjk->rik/dot_general | solution.py:19
  9.9 0.2 fusion.111
  10.1 0.8 %slice_convert_fusion.3 = (f32[1,256]{1,0:T(1,128)S(1)}, f32[1,256]{1,0:T(1,128)S(1)}, f32[1,256]{1,0:T(1,128)S(1)}, f32[1,256]{1,0:T(1,128)S(1)}) fusion(bf16[4,256]{1,0:T(4,128)(2,1)} %param.24), kind=kLoop, calls=%fused_computation.173 | loop fusion | flops 1024 | bytes 6144 | tf_op jit(solution)/shard_map/convert_element_type | solution.py:26
  11.0 0.7 copy.67
  11.6 0.2 fusion.112
  11.9 0.2 fusion.114
  12.0 0.9 %fusion.35 = f32[4,32,32]{2,1,0:T(8,128)S(1)} fusion(s32[4,32]{1,0:T(4,128)} %param.29, f32[32,32]{1,0:T(8,128)S(1)} %fusion.50), kind=kOutput, calls=%fused_computation.77 | convolution fusion | flops 1576960 | bytes 20992 | tf_op jit(solution)/shard_map/rij,rjk->rik/dot_general | solution.py:19
  13.0 0.2 fusion.30
  13.2 0.2 fusion.47
  13.4 0.2 fusion.113
  13.6 0.2 fusion.115
  13.8 0.6 broadcast_compare_fusion
  15.1 0.2 convolution_bitcast_fusion.2
  15.3 3.1 %collective-permute-start = (bf16[4,32,256]{2,1,0:T(8,128)(2,1)S(1)}, bf16[4,32,256]{2,1,0:T(8,128)(2,1)S(1)}, u32[]{:S(2)}, u32[]{:S(2)}) collective-permute-start(bf16[4,32,256]{2,1,0:T(8,128)(2,1)S(1)} %multiply_convert_fusion.4), channel_id=1, source_target_pairs={{0,1},{1,0},{2,3},{3,2},{4,5},{5,4},{6,7},{7,6},{8,9},{9,8},{10,11... | collective-permute-start | bytes 196616 | tf_op jit(solution)/shard_map/ppermute | solution.py:15
  18.6 0.2 fusion.32
  18.8 0.2 fusion.60
  19.0 0.2 fusion.45
  19.3 0.7 fusion.57
  20.1 0.2 fusion.51
  20.3 0.7 fusion.52
  21.0 0.7 fusion.58
  21.8 0.8 fusion.53
  22.5 0.3 convolution_bitcast_fusion
  22.8 0.6 convert_bitcast_fusion.5
  23.4 0.6 convert_bitcast_fusion.4
  24.0 0.2 reduce-window.17
  24.2 0.5 add_bitcast_fusion
  24.8 0.7 reshape.257
  25.4 0.7 reshape.258
  26.1 0.7 reshape.260
  26.8 0.7 reshape.259
  27.6 0.3 fusion.48
  27.9 0.2 fusion.65
  28.0 0.6 exp.39
  28.6 0.7 fusion.54
  29.3 0.6 copy.177
  29.9 0.6 copy.176
  31.4 1.2 %multiply_convert_fusion.2 = bf16[4,32,8,64]{3,1,2,0:T(8,128)(2,1)S(1)} fusion(f32[4,32,8,64]{3,2,1,0:T(8,128)S(1)} %squeeze.35, f32[4,32,8,64]{3,2,1,0:T(8,128)S(1)} %squeeze.34, f32[4,32,8,64]{3,2,1,0:T(8,128)S(1)} %squeeze.33, f32[4,32,8,64]{3,2,1,0:T(8,128)S(1)} %squeeze.32, f32[8,64]{1,0:T(8,128)} %reshape.260, f32[8,64]{1,0:T(8,128)} %reshape.259, ...), kind=kLoop, calls=%fused_computation.30 | loop fusion | flops 786432 | bytes 1187840 | tf_op jit(solution)/shard_map/convert_element_type | solution.py:29
  32.6 0.7 pad_maximum_fusion.18
  33.3 2.1 %fusion.4 = f32[4,8,64,256]{3,2,1,0:T(8,128)S(1)} fusion(bf16[4,32,8,64]{3,1,2,0:T(8,128)(2,1)S(1)} %multiply_convert_fusion.2, f32[4,32,8]{1,2,0:T(8,128)} %get-tuple-element.24, bf16[4,32,256]{2,1,0:T(8,128)(2,1)S(1)} %multiply_convert_fusion.4, bf16[4,32,256]{2,1,0:T(8,128)(2,1)S(1)} %collective-permute-done, pred[]{:T(512)S(6)} %eq.180), kind=kOutput, calls=%fused_computation.19 | convolution fusion | flops 201490432 | bytes 2363393 | tf_op jit(solution)/shard_map/rjhp,rjn->rhpn/dot_general | solution.py:124
  35.4 0.3 add_convert_fusion
  35.8 0.8 %copy.99 = bf16[1,4,512,256]{3,1,2,0:T(4,128)(2,1)S(1)} copy(bf16[1,4,512,256]{3,2,1,0:T(8,128)(2,1)S(1)} %bitcast.198) | data formatting | bytes 2097152
  36.7 1.5 %fusion = bf16[1,2,133376]{2,1,0:T(2,128)(2,1)} fusion(pred[4]{0:T(512)(128)(4,1)S(1)} %copy-done.30, s32[4]{0:T(128)S(1)} %copy-done.31, bf16[4,768]{1,0:T(4,128)(2,1)S(1)} %bitcast.217, bf16[4,1536]{1,0:T(4,128)(2,1)S(1)} %bitcast.212, bf16[4,131072]{1,0:T(4,128)(2,1)S(1)} %bitcast.200), kind=kOutput, calls=%fused_computation.3 | convolution fusion | flops 5601808 | bytes 1600532 | tf_op jit(solution)/shard_map/dot_general | solution.py:155
  38.3 0.2 reduce-window.16
  38.5 0.2 reduce_window_sum.31
  39.0 0.2 reduce_window_sum.32
  39.2 0.7 mul.203
  40.0 0.5 select_reduce_fusion.1
  40.5 0.6 broadcast_compare_fusion.4
  41.2 1.1 %convolution_bitcast_fusion.1 = f32[4,32,8,64]{3,1,2,0:T(8,128)S(1)} fusion(bf16[4,32,8,64]{3,1,2,0:T(8,128)(2,1)S(1)} %multiply_convert_fusion.2, f32[4,32,8]{1,2,0:T(8,128)} %copy-done.4, f32[4,32,8]{1,2,0:T(8,128)S(1)} %fusion.48, f32[4,32,32]{2,1,0:T(8,128)S(1)} %fusion.43, pred[4,32,32]{2,1,0:T(8,128)(4,1)} %get-tuple-element.18), kind=kOutput, calls=%fused_computation.11 | convolution fusion | flops 4390912 | bytes 421888 | tf_op jit(solution)/shard_map/rijh,rjhp->rihp/dot_general | solution.py:100
  42.4 0.6 fusion.28
  42.9 1.2 %multiply_reduce_fusion = (f32[4,32]{1,0:T(4,128)S(1)}, f32[4,32,8,64]{3,1,2,0:T(8,128)S(1)}) fusion(f32[4,32,8,64]{3,2,1,0:T(8,128)S(1)} %reshape.266, bf16[4,32,8,64]{3,1,2,0:T(8,128)(2,1)S(1)} %multiply_convert_fusion.2, f32[8]{0:T(128)} %param.27, f32[4,32,8,64]{3,1,2,0:T(8,128)S(1)} %convolution_bitcast_fusion.1, f32[4,32,8,64]{3,1,2,0:T(8,128)S(1)} %fusion.28, ...), kind=kLoop, calls=%fused_computation.28 | loop fusion | flops 786304 | bytes 1184288 | tf_op jit(solution)/shard_map/reduce_sum | solution.py:108
  44.2 0.7 convolution_convert_fusion.2
  44.9 2.8 %collective-permute-done.1 = f32[4,32]{1,0:T(4,128)S(1)} collective-permute-done((f32[4,32]{1,0:T(4,128)S(1)}, f32[4,32]{1,0:T(4,128)S(1)}, u32[]{:S(2)}, u32[]{:S(2)}) %collective-permute-start.1) | collective-permute-done | bytes 544 | tf_op jit(solution)/shard_map/ppermute | solution.py:15
  48.0 0.9 %reshape.247 = bf16[128,512]{1,0:T(8,128)(2,1)} reshape(bf16[4,32,8,64]{3,2,1,0:T(8,128)(2,1)S(1)} %copy.75) | data formatting | bytes 262144 | tf_op jit(solution)/shard_map/reshape | solution.py:116
  48.9 12.5 %all-gather.3.cloned.1.call-done = bf16[4,2,133376]{2,1,0:T(2,128)(2,1)} async-done(((bf16[1,2,133376]{2,1,0:T(2,128)(2,1)}), bf16[4,2,133376]{2,1,0:T(2,128)(2,1)}) %all-gather.3.cloned.1.call-update) | async-done | bytes 2134032 | tf_op jit(solution)/shard_map/all_gather | solution.py:167
  61.4 2.4 %reshape.270 = bf16[8,133376]{1,0:T(8,128)(2,1)S(1)} reshape(bf16[4,2,133376]{2,1,0:T(2,128)(2,1)} %all-gather.3.cloned.1.call-done) | data formatting | bytes 4268032
  63.9 0.7 convolution_convert_fusion
  64.6 1.0 %fusion.1 = bf16[6,131072]{1,0:T(8,128)(2,1)S(1)} fusion(bf16[4,133376]{1,0:T(4,128)(2,1)S(1)} %convolution_convert_fusion, bf16[2,133376]{1,0:T(2,128)(2,1)S(1)} %convolution_convert_fusion.2), kind=kLoop, calls=%fused_computation.8 | loop fusion | flops 3145728 | bytes 3173376 | tf_op jit(solution)/shard_map/concatenate | solution.py:171
  65.7 0.6 reshape.256
  66.3 0.6 reshape.255
  66.9 1.5 %copy.100 = bf16[1,6,512,256]{3,2,1,0:T(8,128)(2,1)} copy(bf16[1,6,512,256]{3,1,2,0:T(8,128)(2,1)S(1)} %bitcast.197) | data formatting | bytes 3145728
  (115 shorter events, 3.3 us)
Async XLA Ops:
  7.2 7.8 %copy-start.3 = (bf16[128,256]{1,0:T(8,128)(2,1)S(1)}, bf16[128,256]{1,0:T(8,128)(2,1)}, u32[]{:S(2)}) copy-start(bf16[128,256]{1,0:T(8,128)(2,1)} %param.17) | copy-start | bytes 196612
  7.2 54.2 %all-gather.3.cloned.1.call-start = ((), (), s32[]{:S(2)}) async-start(), calls=%async_computation | async-start | bytes 2667520 | tf_op jit(solution)/shard_map/all_gather | solution.py:167
  10.1 8.3 %copy-start.28 = (s32[4]{0:T(128)S(1)}, s32[4]{0:T(128)}, u32[]{:S(2)}) copy-start(s32[4]{0:T(128)} %param.30) | copy-start | bytes 52
  11.8 7.4 %copy-start.8 = (bf16[4,3,512]{2,0,1:T(4,128)(2,1)S(1)}, bf16[4,3,512]{2,0,1:T(4,128)(2,1)}, u32[]{:S(2)}) copy-start(bf16[4,3,512]{2,0,1:T(4,128)(2,1)} %param.20) | copy-start | bytes 36868
  13.0 7.2 %copy-start.2 = (bf16[128,512]{1,0:T(8,128)(2,1)S(1)}, bf16[128,512]{1,0:T(8,128)(2,1)}, u32[]{:S(2)}) copy-start(bf16[128,512]{1,0:T(8,128)(2,1)} %param.16) | copy-start | bytes 393220
  15.0 7.8 %copy-start.29 = (f32[8]{0:T(128)S(1)}, f32[8]{0:T(128)}, u32[]{:S(2)}) copy-start(f32[8]{0:T(128)} %param.26) | copy-start | bytes 100
  15.0 7.8 %copy-start.22 = (s32[16]{0:T(128)S(1)}, s32[16]{0:T(128)}, u32[]{:S(2)}) copy-start(s32[16]{0:T(128)} %param.31) | copy-start | bytes 196
  15.0 9.7 %copy-start.6 = (bf16[4,512]{1,0:T(4,128)(2,1)S(1)}, bf16[4,512]{1,0:T(4,128)(2,1)}, u32[]{:S(2)}) copy-start(bf16[4,512]{1,0:T(4,128)(2,1)} %param.23) | copy-start | bytes 12292
  15.0 12.4 %copy-start.20 = (bf16[128,8]{0,1:T(8,128)(2,1)S(1)}, bf16[128,8]{0,1:T(8,128)(2,1)}, u32[]{:S(2)}) copy-start(bf16[128,8]{0,1:T(8,128)(2,1)} %param.19) | copy-start | bytes 6148
  15.0 12.5 %copy-start.18 = (f32[8]{0:T(128)S(1)}, f32[8]{0:T(128)}, u32[]{:S(2)}) copy-start(f32[8]{0:T(128)} %param.25) | copy-start | bytes 100
  15.3 17.9 %collective-permute-start = (bf16[4,32,256]{2,1,0:T(8,128)(2,1)S(1)}, bf16[4,32,256]{2,1,0:T(8,128)(2,1)S(1)}, u32[]{:S(2)}, u32[]{:S(2)}) collective-permute-start(bf16[4,32,256]{2,1,0:T(8,128)(2,1)S(1)} %multiply_convert_fusion.4), channel_id=1, source_target_pairs={{0,1},{1,0},{2,3},{3,2},{4,5},{5,4},{6,7},{7,6},{8,9},{9,8},{10,11... | collective-permute-start | bytes 196616 | tf_op jit(solution)/shard_map/ppermute | solution.py:15
  23.4 0.8 %copy-start.25 = (pred[4]{0:T(512)(128)(4,1)}, pred[4]{0:T(512)(128)(4,1)S(1)}, u32[]{:S(2)}) copy-start(pred[4]{0:T(512)(128)(4,1)S(1)} %get-tuple-element.13) | copy-start | bytes 16
  27.6 2.3 %copy-start.4 = (f32[4,32,8]{1,2,0:T(8,128)}, f32[4,32,8]{1,2,0:T(8,128)S(1)}, u32[]{:S(2)}) copy-start(f32[4,32,8]{1,2,0:T(8,128)S(1)} %compare_select_fusion) | copy-start | bytes 12292
  30.6 0.7 copy-start.16
  30.6 0.7 copy-start.17
  30.6 0.7 copy-start.12
  30.6 0.7 copy-start.13
  30.6 0.7 copy-start.7
  31.4 5.2 %copy-start.9 = (bf16[4,3,512]{2,0,1:T(4,128)(2,1)}, bf16[4,3,512]{2,0,1:T(4,128)(2,1)S(1)}, u32[]{:S(2)}) copy-start(bf16[4,3,512]{2,0,1:T(4,128)(2,1)S(1)} %pad_maximum_fusion.13) | copy-start | bytes 36868
  31.4 4.0 %copy-start = (bf16[4,8,64,256]{3,2,1,0:T(8,128)(2,1)S(1)}, bf16[4,8,64,256]{3,2,1,0:T(8,128)(2,1)}, u32[]{:S(2)}) copy-start(bf16[4,8,64,256]{3,2,1,0:T(8,128)(2,1)} %param.22) | copy-start | bytes 3145732
  31.4 4.0 %copy-start.11 = (f32[4,8]{1,0:T(4,128)S(1)}, f32[4,8]{1,0:T(4,128)}, u32[]{:S(2)}) copy-start(f32[4,8]{1,0:T(4,128)} %exp.39) | copy-start | bytes 388
  33.2 3.3 %copy-start.14 = (bf16[4,3,256]{2,0,1:T(4,128)(2,1)}, bf16[4,3,256]{2,0,1:T(4,128)(2,1)S(1)}, u32[]{:S(2)}) copy-start(bf16[4,3,256]{2,0,1:T(4,128)(2,1)S(1)} %pad_maximum_fusion.18) | copy-start | bytes 18436
  35.7 0.9 %copy-start.30 = (pred[4]{0:T(512)(128)(4,1)S(1)}, pred[4]{0:T(512)(128)(4,1)}, u32[]{:S(2)}) copy-start(pred[4]{0:T(512)(128)(4,1)} %get-tuple-element.35) | copy-start | bytes 16
  35.7 0.9 %copy-start.31 = (s32[4]{0:T(128)S(1)}, s32[4]{0:T(128)}, u32[]{:S(2)}) copy-start(s32[4]{0:T(128)} %add_bitcast_fusion) | copy-start | bytes 52
  36.6 1.6 %copy-start.23 = (s32[16]{0:T(128)S(1)}, s32[16]{0:T(128)}, u32[]{:S(2)}) copy-start(s32[16]{0:T(128)} %param.31) | copy-start | bytes 196
  36.6 1.7 %copy-start.27 = (s32[4,1]{0,1:T(1,128)S(1)}, s32[4,1]{0,1:T(1,128)}, u32[]{:S(2)}) copy-start(s32[4,1]{0,1:T(1,128)} %get-tuple-element.12) | copy-start | bytes 52
  36.6 2.5 %copy-start.21 = (f32[512]{0:T(512)S(1)}, f32[512]{0:T(512)}, u32[]{:S(2)}) copy-start(f32[512]{0:T(512)} %param.28) | copy-start | bytes 6148
  36.7 3.2 %copy-start.1 = (bf16[128,512]{1,0:T(8,128)(2,1)S(1)}, bf16[128,512]{1,0:T(8,128)(2,1)}, u32[]{:S(2)}) copy-start(bf16[128,512]{1,0:T(8,128)(2,1)} %param.18) | copy-start | bytes 393220
  42.3 1.9 %copy-start.10 = (bf16[4,3,512]{2,0,1:T(4,128)(2,1)S(1)}, bf16[4,3,512]{2,0,1:T(4,128)(2,1)}, u32[]{:S(2)}) copy-start(bf16[4,3,512]{2,0,1:T(4,128)(2,1)} %copy-done.9) | copy-start | bytes 36868
  42.3 1.9 %copy-start.15 = (bf16[4,3,256]{2,0,1:T(4,128)(2,1)S(1)}, bf16[4,3,256]{2,0,1:T(4,128)(2,1)}, u32[]{:S(2)}) copy-start(bf16[4,3,256]{2,0,1:T(4,128)(2,1)} %copy-done.14) | copy-start | bytes 18436
  42.3 1.9 %copy-start.26 = (pred[4]{0:T(512)(128)(4,1)S(1)}, pred[4]{0:T(512)(128)(4,1)}, u32[]{:S(2)}) copy-start(pred[4]{0:T(512)(128)(4,1)} %copy-done.25) | copy-start | bytes 16
  44.1 3.7 %copy-start.5 = (f32[8,64]{1,0:T(8,128)S(1)}, f32[8,64]{1,0:T(8,128)}, u32[]{:S(2)}) copy-start(f32[8,64]{1,0:T(8,128)} %mul.203) | copy-start | bytes 6148
  44.1 3.7 %collective-permute-start.1 = (f32[4,32]{1,0:T(4,128)S(1)}, f32[4,32]{1,0:T(4,128)S(1)}, u32[]{:S(2)}, u32[]{:S(2)}) collective-permute-start(f32[4,32]{1,0:T(4,128)S(1)} %get-tuple-element.16), channel_id=1, source_target_pairs={{0,1},{1,0},{2,3},{3,2},{4,5},{5,4},{6,7},{7,6},{8,9},{9,8},{10,11... | collective-permute-start | bytes 1544 | tf_op jit(solution)/shard_map/ppermute | solution.py:15
  48.9 14.9 %copy-start.19 = (s32[8]{0:T(128)S(1)}, s32[8]{0:T(128)}, u32[]{:S(2)}) copy-start(s32[8]{0:T(128)} %select_reduce_fusion.1) | copy-start | bytes 100
  48.9 14.9 %copy-start.24 = (pred[8]{0:T(512)(128)(4,1)S(1)}, pred[8]{0:T(512)(128)(4,1)}, u32[]{:S(2)}) copy-start(pred[8]{0:T(512)(128)(4,1)} %broadcast_compare_fusion.4) | copy-start | bytes 28
Sparse Core Ops, SparseCore 0:
  38.3 23.0 all-gather.2
where the time goes:
time: 76 us; the launch traced here: 75.2 us
  matrix products  15.8 us (21%)
  waiting for transfers between devices  15.4 us (20%)
  between operations  14.7 us (19%)
  local copies, waits for them, and re-layouts  14.1 us (19%)
  other arithmetic  12 us (16%)
  starting transfers between devices  3.23 us (4%)
    all_gather x1, waiting for transfers between devices, body(): lax.all_gather(packed, 'dp', axis=0, tiled=True)  12.5 us
    unnamed x69, local copies, waits for them, and re-layouts  5.66 us
    dot_general x10, matrix products, chain_product(): jnp.einsum('rij,rjk->rik', left, right, precision=lax.Precision.HIGHEST)  4.11 us
    dot_general x6, matrix products, latest_taps(): jnp.einsum('rj,rjc->rc', row, combined, preferred_element_type=jnp.float32)  3.24 us
    ppermute x2, starting transfers between devices, from_partner(): lax.ppermute(x, axis, [(i, i ^ 1 << distance) for i in range(lax.axis_siz...  3.19 us
    ppermute x2, waiting for transfers between devices, from_partner(): lax.ppermute(x, axis, [(i, i ^ 1 << distance) for i in range(lax.axis_siz...  2.83 us
    dot_general x1, matrix products, body(): jnp.einsum('rjhp,rjn->rhpn', scaled_x, b_act.astype(jnp.float32), precisi...  2.11 us
    convert_element_type x3, local copies, waits for them, and re-layouts, convolve(): summed = summed + weight[k].astype(jnp.float32) * tapped[k]  1.99 us
  transfers between devices with their start and end apart: 3, of which 2 were waited for; matrix products, arithmetic and copies ran while one was open for 29% of the time, Pallas kernels for 0%

commit v1 on v0

v1 whole, which is shorter than its diff:
```python
import functools

import jax
import jax.numpy as jnp
from jax import lax
from jax.experimental import pallas as pl
from jax.experimental.pallas import tpu as pltpu
from jax.sharding import PartitionSpec as P

P_SIZE = 64
N = 256
NODES = 32
MOVE = 2
IN_CAP = 4
KEEP = 6
CHUNKS = 4
MESH = pl.DeviceIdType.MESH
F32 = jnp.float32
BF16 = jnp.bfloat16


def mm(a, b):
    return jnp.dot(a.astype(BF16), b.astype(BF16), preferred_element_type=F32)


def mm_exact(a, b):
    return jnp.dot(a, b, preferred_element_type=F32, precision=lax.Precision.HIGHEST)


def iota(shape, dim):
    return lax.broadcasted_iota(jnp.int32, shape, dim)


def silu(v):
    return v / (1.0 + jnp.exp(-v))


def kernel(
    n_dp,
    x_ref,
    bc_ref,
    gate_ref,
    dt_ref,
    hx_ref,
    hbc_ref,
    ssm_ref,
    wx_ref,
    wbc_ref,
    bias_ref,
    rate_ref,
    skip_ref,
    gain_ref,
    par_ref,
    acc_ref,
    dst_ref,
    y_ref,
    new_ref,
    ncx_ref,
    ncbc_ref,
    hist_x,
    hist_bc,
    own_bc,
    other_bc,
    sq_own,
    sq_other,
    taps,
    *rest,
):
    bufs = rest[:CHUNKS]
    t_send, t_recv, x_send, x_recv, p_send, p_recv = rest[CHUNKS:]
    chips = n_dp // 2
    me = lax.axis_index("dp")
    chip = me // 2
    core = me % 2
    tensor = lax.axis_index("tensor")
    parity = tensor % 2
    mate = tensor + 1 - 2 * parity
    twin = me + 1 - 2 * core

    def ahead(j):
        return 2 * ((chip + j) % chips) + core

    def behind(j, which):
        return 2 * ((chip + chips - j) % chips) + which

    barrier = pltpu.get_barrier_semaphore()
    pl.semaphore_signal(barrier, inc=1, device_id={"tensor": mate}, device_id_type=MESH)
    pl.semaphore_signal(barrier, inc=1, device_id={"dp": twin}, device_id_type=MESH)
    for j in range(1, chips):
        pl.semaphore_signal(barrier, inc=1, device_id={"dp": ahead(j)}, device_id_type=MESH)

    requests = par_ref.shape[0]
    rows = x_ref.shape[0]
    heads = dt_ref.shape[1]
    width = x_ref.shape[1]

    stay = [jnp.int32(0)] * (requests - MOVE)
    move = [jnp.int32(0)] * MOVE
    stay_count = jnp.int32(0)
    move_count = jnp.int32(0)
    for q in range(requests):
        staying = dst_ref[me * requests + q] < 0
        for k in range(requests - MOVE):
            stay[k] = jnp.where(staying & (stay_count == k), q, stay[k])
        for k in range(MOVE):
            move[k] = jnp.where(jnp.logical_not(staying) & (move_count == k), q, move[k])
        stay_count = stay_count + jnp.where(staying, 1, 0)
        move_count = move_count + jnp.where(staying, 0, 1)
    source = [jnp.int32(-1)] * IN_CAP
    arrived = jnp.int32(0)
    for d in range(n_dp):
        rank = jnp.int32(0)
        for q in range(requests):
            to = dst_ref[d * requests + q]
            mine = to == me
            for k in range(IN_CAP):
                source[k] = jnp.where(mine & (arrived == k), d * MOVE + rank, source[k])
            arrived = arrived + jnp.where(mine, 1, 0)
            rank = rank + jnp.where(to >= 0, 1, 0)

    row = iota((rows, rows), 0)
    col = iota((rows, rows), 1)
    tile = (iota((NODES, rows), 1) % NODES == iota((NODES, rows), 0)).astype(F32)
    tiled = mm(par_ref[...].astype(F32), tile)
    owner = iota((requests, rows), 0)
    flat = jnp.where(tiled < -0.5, -1.0, tiled + (NODES * owner).astype(F32))
    flat = jnp.sum(
        jnp.where(iota((requests, rows), 1) // NODES == owner, flat, 0.0), axis=0, keepdims=True
    )
    hop_t = jnp.where(row.astype(F32) == flat, 1.0, 0.0)
    eye = jnp.where(row == col, 1.0, 0.0)
    hop1 = hop_t.T
    hop2 = mm(hop1, hop1)
    hop3 = mm(hop2, hop1)
    hop4 = mm(hop2, hop2)
    hop8 = mm(hop4, hop4)
    hop16 = mm(hop8, hop8)
    path = eye + hop1
    path = path + mm(hop2, path)
    path = path + mm(hop4, path)
    path = path + mm(hop8, path)
    path = path + mm(hop16, path)
    depth = jnp.sum(path, axis=1, keepdims=True) - 1.0
    hops = [eye, hop1, hop2, hop3]
    hist_rows = 8 * requests
    hist_row = iota((rows, hist_rows), 1)
    hist_mine = (hist_row // 8 == iota((rows, hist_rows), 0) // NODES) & (hist_row % 8 < 3)
    lags = [
        jnp.where(hist_mine & ((hist_row % 8).astype(F32) == 3.0 - k + depth), 1.0, 0.0)
        for k in range(4)
    ]

    hist_x[...] = jnp.zeros(hist_x.shape, F32)
    hist_bc[...] = jnp.zeros(hist_bc.shape, F32)
    for r in range(requests):
        hist_x[8 * r : 8 * r + 3, :] = hx_ref[r].astype(F32)
        hist_bc[8 * r : 8 * r + 3, :] = hbc_ref[r].astype(F32)

    def convolve(values, history, w_ref):
        summed = w_ref[0:1, :].astype(F32) * values.astype(F32)
        for k in range(1, 4):
            tap = mm(hops[k], values) + mm(lags[k], history)
            summed = summed + w_ref[k : k + 1, :].astype(F32) * tap
        return silu(summed).astype(BF16)

    own_bc[...] = convolve(bc_ref[...], hist_bc[...], wbc_ref)

    pl.semaphore_wait(barrier, 1 + chips)
    bc_copy = pltpu.make_async_remote_copy(
        src_ref=own_bc,
        dst_ref=other_bc,
        send_sem=t_send.at[0],
        recv_sem=t_recv.at[0],
        device_id={"tensor": mate},
        device_id_type=MESH,
    )
    bc_copy.start()

    x_act = convolve(x_ref[...], hist_x[...], wx_ref)

    raw = dt_ref[...].astype(F32) + bias_ref[...]
    step = jnp.maximum(raw, 0.0) + jnp.log1p(jnp.exp(-jnp.abs(raw)))
    step_decay = -rate_ref[...] * step
    log = mm_exact(path, step_decay)

    target = jnp.zeros((rows, rows), jnp.int32)
    for r in range(requests):
        target = jnp.where(row // NODES == r, NODES * r + acc_ref[r], target)
    accept_hot = jnp.where(col == target, 1.0, 0.0)
    accept_log = mm_exact(accept_hot, log)
    accept_path = jnp.sum(accept_hot * path.T, axis=1, keepdims=True) > 0.5
    reach = jnp.where(accept_path, accept_log - log, -1e30)
    coef = (jnp.where(accept_path, jnp.exp(reach), 0.0) * step).astype(BF16).astype(F32)
    accept_exp = jnp.exp(accept_log)

    lane_low = iota((1, 2 * P_SIZE), 1) < P_SIZE

    def expand(v):
        return jnp.concatenate(
            [
                jnp.where(lane_low, v[:, 2 * q : 2 * q + 1], v[:, 2 * q + 1 : 2 * q + 2])
                for q in range(heads // 2)
            ],
            axis=1,
        )

    x_float = x_act.astype(F32)
    scaled_t = (expand(coef) * x_float).T.astype(BF16)

    def tap_rows():
        pick = iota((8 * requests, rows), 0)
        ids = stay + move
        wanted = jnp.zeros((8 * requests, rows), jnp.int32)
        for k in range(requests):
            wanted = jnp.where(pick // 8 == k, NODES * ids[k] + acc_ref[ids[k]], wanted)
        hot = jnp.where(iota((8 * requests, rows), 1) == wanted, 1.0, 0.0)
        turn = pick % 8
        node_part = jnp.where(
            turn == 2, hot, jnp.where(turn == 1, mm(hot, hops[1]), mm(hot, hops[2]))
        )
        turn = iota((8 * requests, hist_rows), 0) % 8
        lag_part = jnp.where(
            turn == 2, 0.0, jnp.where(turn == 1, mm(hot, lags[1]), mm(hot, lags[2]))
        )
        fx = mm(node_part, x_ref[...]) + mm(lag_part, hist_x[...])
        fbc = mm(node_part, bc_ref[...]) + mm(lag_part, hist_bc[...])
        return fx.astype(BF16), fbc.astype(BF16)

    fresh_x, fresh_bc = tap_rows()
    stays = requests - MOVE
    taps[me] = jnp.concatenate([fresh_x[8 * stays :], fresh_bc[8 * stays :]], axis=1)
    for k in range(stays):
        ncx_ref[k] = fresh_x[8 * k : 8 * k + 3]
        ncbc_ref[k] = fresh_bc[8 * k : 8 * k + 3]

    bc_copy.wait()
    own = own_bc[...]
    other = other_bc[...]
    even = (parity == 0).astype(F32)
    own_f = own.astype(F32)
    other_f = other.astype(F32)
    b_act = (even * own_f + (1.0 - even) * other_f).astype(BF16)
    c_act = (even * other_f + (1.0 - even) * own_f).astype(BF16)

    row_request = iota((rows, 1), 0) // NODES
    first_row = iota((rows, 1), 0)
    per = heads // CHUNKS
    depth_rows = per * P_SIZE

    def fresh_of(request):
        b_mine = jnp.where(row_request == request, b_act.astype(F32), 0.0).astype(BF16)
        scale = jnp.sum(
            jnp.where(first_row == NODES * request, accept_exp, 0.0), axis=0, keepdims=True
        )

        def chunk(c):
            update = mm(scaled_t[c * depth_rows : (c + 1) * depth_rows], b_mine)
            parts = []
            for h in range(per):
                head = c * per + h
                held = ssm_ref[request, head].astype(F32) * scale[:, head : head + 1]
                parts.append(held + update[h * P_SIZE : (h + 1) * P_SIZE])
            return jnp.concatenate(parts, axis=0).astype(BF16)

        return chunk

    def block_of(c, device):
        if c == CHUNKS:
            return taps.at[device]
        return bufs[c].at[pl.ds(device * MOVE, MOVE)]

    def across(c, j, device):
        return pltpu.make_async_remote_copy(
            src_ref=block_of(c, device),
            dst_ref=block_of(c, device),
            send_sem=x_send.at[c, j],
            recv_sem=x_recv.at[c, j],
            device_id={"dp": ahead(j)},
            device_id_type=MESH,
        )

    def beside(c, j, device):
        return pltpu.make_async_remote_copy(
            src_ref=block_of(c, device),
            dst_ref=block_of(c, device),
            send_sem=p_send.at[c, j],
            recv_sem=p_recv.at[c, j],
            device_id={"dp": twin},
            device_id_type=MESH,
        )

    def send(c):
        for j in range(1, chips):
            across(c, j, me).start()
        beside(c, 0, me).start()

    def relay(c):
        for j in range(1, chips):
            across(c, j, behind(j, core)).wait_recv()
            beside(c, j, behind(j, core)).start()

    def place(c):
        for j in range(chips):
            beside(c, j, behind(j, 1 - core)).wait_recv()
        for k in range(IN_CAP):
            index = jnp.maximum(source[k], 0)
            there = source[k] >= 0
            if c == CHUNKS:
                found = taps[index // MOVE].astype(F32)
                found = jnp.where(index % MOVE == 0, found[0:8], found[8:16])
                found = jnp.where(there, found, 0.0).astype(BF16)
                ncx_ref[stays + k] = found[0:3, :width]
                ncbc_ref[stays + k] = found[0:3, width:]
            else:
                found = jnp.where(there, bufs[c][index].astype(F32), 0.0).astype(BF16)
                new_ref[stays + k, c * per : (c + 1) * per] = found.reshape(per, P_SIZE, N)

    movers = [fresh_of(move[k]) for k in range(MOVE)]
    for c in range(CHUNKS):
        for k in range(MOVE):
            bufs[c][me * MOVE + k] = movers[k](c)
        send(c)
    send(CHUNKS)

    inner = lax.dot_general(
        c_act, b_act, (((1,), (1,)), ((), ())), preferred_element_type=F32
    )
    inside = path > 0.5
    inner = jnp.where(inside, inner, 0.0)
    log_t = log.T
    step_t = step.T
    log_exp = expand(jnp.exp(log))
    held = jnp.concatenate(
        [
            lax.dot_general(
                c_act[NODES * r : NODES * (r + 1)],
                ssm_ref[r].reshape(width, N),
                (((1,), (1,)), ((), ())),
                preferred_element_type=F32,
            )
            for r in range(requests)
        ],
        axis=0,
    )
    tree = []
    for q in range(heads // 2):
        pair = x_act[:, 2 * P_SIZE * q : 2 * P_SIZE * (q + 1)]
        both = []
        for h in (2 * q, 2 * q + 1):
            spread = jnp.where(inside, log[:, h : h + 1] - log_t[h : h + 1, :], -1e30)
            weight = inner * jnp.exp(spread) * step_t[h : h + 1, :]
            both.append(mm(weight, pair))
        tree.append(jnp.where(lane_low, both[0], both[1]))
    tree = jnp.concatenate(tree, axis=1)
    mixed = tree + held * log_exp + expand(skip_ref[...]) * x_float
    gated = mixed * silu(gate_ref[...].astype(F32))
    squares = jnp.sum(gated * gated, axis=1, keepdims=True)
    sq_own[...] = jnp.broadcast_to(
        jnp.sum(jnp.where(row == col, squares, 0.0), axis=0, keepdims=True), sq_own.shape
    )
    sq_copy = pltpu.make_async_remote_copy(
        src_ref=sq_own,
        dst_ref=sq_other,
        send_sem=t_send.at[1],
        recv_sem=t_recv.at[1],
        device_id={"tensor": mate},
        device_id_type=MESH,
    )
    sq_copy.start()

    relay(0)
    for k in range(stays):
        chunk = fresh_of(stay[k])
        for c in range(CHUNKS):
            new_ref[k, c * per : (c + 1) * per] = chunk(c).reshape(per, P_SIZE, N)

    sq_copy.wait()
    partner = jnp.sum(jnp.where(row == col, sq_other[0:1, :], 0.0), axis=1, keepdims=True)
    mean_square = (squares + partner) * (1.0 / (2 * heads * P_SIZE))
    y_ref[...] = (gated * lax.rsqrt(mean_square + 1e-05) * gain_ref[...]).astype(BF16)

    for c in range(1, CHUNKS + 1):
        relay(c)
        place(c - 1)
    place(CHUNKS)
    for c in range(CHUNKS + 1):
        for j in range(1, chips):
            across(c, j, me).wait_send()
        for j in range(chips):
            beside(c, j, behind(j, core)).wait_send()


def body(
    x_stream,
    bc_stream,
    gate_stream,
    dt_stream,
    conv_x_state,
    conv_bc_state,
    ssm_state,
    conv_x_weight,
    conv_bc_weight,
    dt_bias,
    decay_rate,
    skip_gain,
    norm_gain,
    parents,
    accepted,
    destination,
):
    n_dp = lax.axis_size("dp")
    chips = n_dp // 2
    rows, width = x_stream.shape
    bc_width = bc_stream.shape[1]
    requests = parents.shape[0]
    heads = dt_stream.shape[1]
    vmem = pl.BlockSpec(memory_space=pltpu.VMEM)
    smem = pl.BlockSpec(memory_space=pltpu.SMEM)
    copies = (CHUNKS + 1, chips)
    return pl.pallas_call(
        functools.partial(kernel, n_dp),
        out_shape=(
            jax.ShapeDtypeStruct((rows, width), BF16),
            jax.ShapeDtypeStruct((KEEP, heads, P_SIZE, N), BF16),
            jax.ShapeDtypeStruct((KEEP, 3, width), BF16),
            jax.ShapeDtypeStruct((KEEP, 3, bc_width), BF16),
        ),
        in_specs=[vmem] * 14 + [smem] * 2,
        out_specs=(vmem,) * 4,
        scratch_shapes=[
            pltpu.VMEM((8 * requests, width), F32),
            pltpu.VMEM((8 * requests, bc_width), F32),
            pltpu.VMEM((rows, bc_width), BF16),
            pltpu.VMEM((rows, bc_width), BF16),
            pltpu.VMEM((8, rows), F32),
            pltpu.VMEM((8, rows), F32),
            pltpu.VMEM((n_dp, 8 * MOVE, width + bc_width), BF16),
        ]
        + [
            pltpu.VMEM((n_dp * MOVE, heads // CHUNKS * P_SIZE, N), BF16) for _ in range(CHUNKS)
        ]
        + [pltpu.SemaphoreType.DMA((2,))] * 2
        + [pltpu.SemaphoreType.DMA(copies)] * 4,
        compiler_params=pltpu.CompilerParams(
            collective_id=0, has_side_effects=True, vmem_limit_bytes=40 << 20
        ),
        name="verify_and_migrate",
    )(
        x_stream,
        bc_stream,
        gate_stream,
        dt_stream,
        conv_x_state,
        conv_bc_state,
        ssm_state,
        conv_x_weight,
        conv_bc_weight,
        dt_bias.reshape(1, heads),
        decay_rate.reshape(1, heads),
        skip_gain.reshape(1, heads),
        norm_gain.reshape(1, width),
        parents,
        accepted,
        destination,
    )


def solution(mesh):
    placed = (
        P(("groups", "dp"), "tensor"),
        P(("groups", "dp"), "tensor"),
        P(("groups", "dp"), "tensor"),
        P(("groups", "dp"), "tensor"),
        P(("groups", "dp"), None, "tensor"),
        P(("groups", "dp"), None, "tensor"),
        P(("groups", "dp"), "tensor", None, None),
        P(None, "tensor"),
        P(None, "tensor"),
        P("tensor"),
        P("tensor"),
        P("tensor"),
        P("tensor"),
        P(("groups", "dp"), None),
        P(("groups", "dp")),
        P("groups"),
    )
    return jax.shard_map(
        body,
        mesh=mesh,
        in_specs=placed,
        out_specs=(
            P(("groups", "dp"), "tensor"),
            P(("groups", "dp"), "tensor", None, None),
            P(("groups", "dp"), None, "tensor"),
            P(("groups", "dp"), None, "tensor"),
        ),
        check_vma=False,
    )
```

time: 76 us -> 38 us (0.50)
  Pallas kernels: 0 us -> 21.8 us
  matrix products: 15.8 us -> 0 us
  waiting for transfers between devices: 15.4 us -> 0 us
  between operations: 14.7 us -> 0.66 us
  other arithmetic: 12 us -> 0 us
  starting transfers between devices: 3.23 us -> 0 us
  local copies, waits for them, and re-layouts: 14.1 us -> 15.1 us
    pallas_call x0 -> x1, Pallas kernels: none -> 21.8 us  [body(): pl.pallas_call(functools.partial(kernel, n_dp), out_shape=(jax.ShapeDtype...]
    dot_general x31 -> x0, matrix products: 15.8 us -> none  [the longest x10 4.11 us: chain_product(): jnp.einsum('rij,rjk->rik', left, right, precision=lax.Precision.HIGHEST)]
    all_gather x1 -> x0, waiting for transfers between devices: 12.5 us -> none  [body(): lax.all_gather(packed, 'dp', axis=0, tiled=True)]
    unnamed x69 -> x33, local copies, waits for them, and re-layouts: 5.66 us -> 15.1 us
    convert_element_type x14 -> x0, other arithmetic: 3.45 us -> none  [the longest x2 1.27 us: convolve(): return jax.nn.silu(summed).astype(jnp.bfloat16)]
    ppermute x2 -> x0, starting transfers between devices: 3.19 us -> none  [from_partner(): lax.ppermute(x, axis, [(i, i ^ 1 << distance) for i in range(lax.axis_siz...]
    convert_element_type x7 -> x0, local copies, waits for them, and re-layouts: 2.98 us -> none  [the longest x3 1.99 us: convolve(): summed = summed + weight[k].astype(jnp.float32) * tapped[k]]
    another operation x11 -> x0, other arithmetic: 2.84 us -> none
  transfers between devices with their start and end apart: 3 -> 0, of which waited for: 2 -> 0; matrix products, arithmetic and copies ran while one was open for 29% -> 0% of each run, Pallas kernels for 0% -> 0%
where the time goes in v1:
time: 38 us; the launch traced here: 37.5 us
  Pallas kernels  21.8 us (57%)
  local copies, waits for them, and re-layouts  15.1 us (40%)
  between operations  0.66 us (2%)
    pallas_call x1, Pallas kernels, body(): pl.pallas_call(functools.partial(kernel, n_dp), out_shape=(jax.ShapeDtype...  21.8 us
    unnamed x33, local copies, waits for them, and re-layouts  15.1 us

profile of v1, /device:TPU:0, one launch (start us, length us, event | category | flops | bytes accessed | tf_op | source)
XLA Modules:
  0.0 37.5 jit_solution(13715901763613411489)
XLA Ops:
  0.6 0.7 %copy.22.hbc_ref = bf16[4,3,256]{2,1,0:T(4,128)(2,1)S(1)} copy(bf16[4,3,256]{2,0,1:T(4,128)(2,1)} %param.21) | data formatting | bytes 12288 | tf_op args[5]
  1.3 0.7 %copy.21.hx_ref = bf16[4,3,512]{2,1,0:T(4,128)(2,1)S(1)} copy(bf16[4,3,512]{2,0,1:T(4,128)(2,1)} %param.20) | data formatting | bytes 24576 | tf_op args[4]
  2.0 0.8 %copy.20.dt_ref = bf16[128,8]{1,0:T(8,128)(2,1)S(1)} copy(bf16[128,8]{0,1:T(8,128)(2,1)} %param.19) | data formatting | bytes 4096 | tf_op args[3]
  2.8 0.0 copy-start
  2.8 1.2 %copy-done = bf16[4,8,64,256]{3,2,1,0:T(8,128)(2,1)S(1)} copy-done((bf16[4,8,64,256]{3,2,1,0:T(8,128)(2,1)S(1)}, bf16[4,8,64,256]{3,2,1,0:T(8,128)(2,1)}, u32[]{:S(2)}) %copy-start) | copy-done | bytes 1048600
  4.1 0.0 copy-start.1
  4.1 0.9 %copy-done.1 = bf16[128,512]{1,0:T(8,128)(2,1)S(1)} copy-done((bf16[128,512]{1,0:T(8,128)(2,1)S(1)}, bf16[128,512]{1,0:T(8,128)(2,1)}, u32[]{:S(2)}) %copy-start.1) | copy-done | bytes 131096
  5.0 0.0 copy-start.2
  5.0 0.9 %copy-done.2 = bf16[128,512]{1,0:T(8,128)(2,1)S(1)} copy-done((bf16[128,512]{1,0:T(8,128)(2,1)S(1)}, bf16[128,512]{1,0:T(8,128)(2,1)}, u32[]{:S(2)}) %copy-start.2) | copy-done | bytes 131096
  5.9 0.0 copy-start.3
  5.9 0.8 %copy-done.3 = bf16[128,256]{1,0:T(8,128)(2,1)S(1)} copy-done((bf16[128,256]{1,0:T(8,128)(2,1)S(1)}, bf16[128,256]{1,0:T(8,128)(2,1)}, u32[]{:S(2)}) %copy-start.3) | copy-done | bytes 65560
  6.7 0.0 copy-start.4
  6.7 0.7 %copy-done.4 = bf16[4,512]{1,0:T(4,128)(2,1)S(1)} copy-done((bf16[4,512]{1,0:T(4,128)(2,1)S(1)}, bf16[4,512]{1,0:T(4,128)(2,1)}, u32[]{:S(2)}) %copy-start.4) | copy-done | bytes 4120
  7.4 0.0 copy-start.5
  7.4 0.7 %copy-done.5 = bf16[4,256]{1,0:T(4,128)(2,1)S(1)} copy-done((bf16[4,256]{1,0:T(4,128)(2,1)S(1)}, bf16[4,256]{1,0:T(4,128)(2,1)}, u32[]{:S(2)}) %copy-start.5) | copy-done | bytes 2072
  8.1 0.0 copy-start.6
  8.1 0.7 %copy-done.6 = f32[512]{0:T(512)S(1)} copy-done((f32[512]{0:T(512)S(1)}, f32[512]{0:T(512)}, u32[]{:S(2)}) %copy-start.6) | copy-done | bytes 2072
  8.8 0.0 copy-start.7
  8.8 0.7 %copy-done.7 = s32[4,32]{1,0:T(4,128)S(1)} copy-done((s32[4,32]{1,0:T(4,128)S(1)}, s32[4,32]{1,0:T(4,128)}, u32[]{:S(2)}) %copy-start.7) | copy-done | bytes 536
  9.4 0.0 copy-start.8
  9.5 0.7 %copy-done.8 = f32[8]{0:T(128)S(1)} copy-done((f32[8]{0:T(128)S(1)}, f32[8]{0:T(128)}, u32[]{:S(2)}) %copy-start.8) | copy-done | bytes 56
  10.1 0.0 copy-start.9
  10.1 0.7 %copy-done.9 = f32[8]{0:T(128)S(1)} copy-done((f32[8]{0:T(128)S(1)}, f32[8]{0:T(128)}, u32[]{:S(2)}) %copy-start.9) | copy-done | bytes 56
  10.8 0.0 copy-start.10
  10.8 0.7 %copy-done.10 = f32[8]{0:T(128)S(1)} copy-done((f32[8]{0:T(128)S(1)}, f32[8]{0:T(128)}, u32[]{:S(2)}) %copy-start.10) | copy-done | bytes 56
  11.4 0.0 copy-start.11
  11.4 0.7 %copy-done.11 = s32[4]{0:T(128)S(1)} copy-done((s32[4]{0:T(128)S(1)}, s32[4]{0:T(128)}, u32[]{:S(2)}) %copy-start.11) | copy-done | bytes 40
  12.1 0.0 copy-start.12
  12.1 0.7 %copy-done.12 = s32[16]{0:T(128)S(1)} copy-done((s32[16]{0:T(128)S(1)}, s32[16]{0:T(128)}, u32[]{:S(2)}) %copy-start.12) | copy-done | bytes 88
  12.7 21.8 %verify_and_migrate.1 = (bf16[128,512]{1,0:T(8,128)(2,1)S(1)}, bf16[6,8,64,256]{3,2,1,0:T(8,128)(2,1)S(1)}, bf16[6,3,512]{2,1,0:T(4,128)(2,1)S(1)}, bf16[6,3,256]{2,1,0:T(4,128)(2,1)S(1)}) custom-call(bf16[128,512]{1,0:T(8,128)(2,1)S(1)} %copy-done.1, bf16[128,256]{1,0:T(8,128)(2,1)S(1)} %copy-done.3, bf16[128,512]{1,0:T(8,128)(2,1)S(1)} %copy-done.2, ...), custom_call_target="tpu_custom_call" | custom-call | tf_op jit(solution)/shard_map/verify_and_migrate/pallas_call | solution.py:420
  34.5 0.7 %copy.27 = bf16[128,512]{1,0:T(8,128)(2,1)} copy(bf16[128,512]{1,0:T(8,128)(2,1)S(1)} %get-tuple-element.8) | data formatting | bytes 262144
  35.2 1.1 %copy.28 = bf16[6,8,64,256]{3,2,1,0:T(8,128)(2,1)} copy(bf16[6,8,64,256]{3,2,1,0:T(8,128)(2,1)S(1)} %get-tuple-element.9) | data formatting | bytes 3145728
  36.3 0.6 %copy.29 = bf16[6,3,512]{2,1,0:T(4,128)(2,1)} copy(bf16[6,3,512]{2,1,0:T(4,128)(2,1)S(1)} %get-tuple-element.10) | data formatting | bytes 36864
  36.9 0.6 %copy.30 = bf16[6,3,256]{2,1,0:T(4,128)(2,1)} copy(bf16[6,3,256]{2,1,0:T(4,128)(2,1)S(1)} %get-tuple-element.11) | data formatting | bytes 18432
Async XLA Ops:
  2.8 1.2 %copy-start = (bf16[4,8,64,256]{3,2,1,0:T(8,128)(2,1)S(1)}, bf16[4,8,64,256]{3,2,1,0:T(8,128)(2,1)}, u32[]{:S(2)}) copy-start(bf16[4,8,64,256]{3,2,1,0:T(8,128)(2,1)} %ssm_ref.1) | copy-start | bytes 3145732
  4.1 0.9 %copy-start.1 = (bf16[128,512]{1,0:T(8,128)(2,1)S(1)}, bf16[128,512]{1,0:T(8,128)(2,1)}, u32[]{:S(2)}) copy-start(bf16[128,512]{1,0:T(8,128)(2,1)} %x_ref.1) | copy-start | bytes 393220
  5.0 0.9 %copy-start.2 = (bf16[128,512]{1,0:T(8,128)(2,1)S(1)}, bf16[128,512]{1,0:T(8,128)(2,1)}, u32[]{:S(2)}) copy-start(bf16[128,512]{1,0:T(8,128)(2,1)} %gate_ref.1) | copy-start | bytes 393220
  5.9 0.8 %copy-start.3 = (bf16[128,256]{1,0:T(8,128)(2,1)S(1)}, bf16[128,256]{1,0:T(8,128)(2,1)}, u32[]{:S(2)}) copy-start(bf16[128,256]{1,0:T(8,128)(2,1)} %bc_ref.1) | copy-start | bytes 196612
  6.7 0.7 %copy-start.4 = (bf16[4,512]{1,0:T(4,128)(2,1)S(1)}, bf16[4,512]{1,0:T(4,128)(2,1)}, u32[]{:S(2)}) copy-start(bf16[4,512]{1,0:T(4,128)(2,1)} %wx_ref.1) | copy-start | bytes 12292
  7.4 0.7 %copy-start.5 = (bf16[4,256]{1,0:T(4,128)(2,1)S(1)}, bf16[4,256]{1,0:T(4,128)(2,1)}, u32[]{:S(2)}) copy-start(bf16[4,256]{1,0:T(4,128)(2,1)} %wbc_ref.1) | copy-start | bytes 6148
  8.1 0.7 %copy-start.6 = (f32[512]{0:T(512)S(1)}, f32[512]{0:T(512)}, u32[]{:S(2)}) copy-start(f32[512]{0:T(512)} %param.28) | copy-start | bytes 6148
  8.8 0.7 %copy-start.7 = (s32[4,32]{1,0:T(4,128)S(1)}, s32[4,32]{1,0:T(4,128)}, u32[]{:S(2)}) copy-start(s32[4,32]{1,0:T(4,128)} %par_ref.1) | copy-start | bytes 1540
  9.4 0.7 %copy-start.8 = (f32[8]{0:T(128)S(1)}, f32[8]{0:T(128)}, u32[]{:S(2)}) copy-start(f32[8]{0:T(128)} %param.25) | copy-start | bytes 100
  10.1 0.7 %copy-start.9 = (f32[8]{0:T(128)S(1)}, f32[8]{0:T(128)}, u32[]{:S(2)}) copy-start(f32[8]{0:T(128)} %param.26) | copy-start | bytes 100
  10.8 0.7 %copy-start.10 = (f32[8]{0:T(128)S(1)}, f32[8]{0:T(128)}, u32[]{:S(2)}) copy-start(f32[8]{0:T(128)} %param.27) | copy-start | bytes 100
  11.4 0.7 %copy-start.11 = (s32[4]{0:T(128)S(1)}, s32[4]{0:T(128)}, u32[]{:S(2)}) copy-start(s32[4]{0:T(128)} %acc_ref.1) | copy-start | bytes 52
  12.1 0.7 %copy-start.12 = (s32[16]{0:T(128)S(1)}, s32[16]{0:T(128)}, u32[]{:S(2)}) copy-start(s32[16]{0:T(128)} %dst_ref.1) | copy-start | bytes 196

commit v2 on v1

--- a/solution.py
+++ b/solution.py
@@ -13,7 +13,10 @@
 MOVE = 2
 IN_CAP = 4
 KEEP = 6
-CHUNKS = 4
+CHUNKS = 8
+RAW = 4
+TAPS, AUX, SCALE = CHUNKS, CHUNKS + 1, CHUNKS + 2
+MESSAGES = CHUNKS + 3
 MESH = pl.DeviceIdType.MESH
 F32 = jnp.float32
 BF16 = jnp.bfloat16
@@ -35,39 +38,37 @@
     return v / (1.0 + jnp.exp(-v))
 
 
-def kernel(
-    n_dp,
-    x_ref,
-    bc_ref,
-    gate_ref,
-    dt_ref,
-    hx_ref,
-    hbc_ref,
-    ssm_ref,
-    wx_ref,
-    wbc_ref,
-    bias_ref,
-    rate_ref,
-    skip_ref,
-    gain_ref,
-    par_ref,
-    acc_ref,
-    dst_ref,
-    y_ref,
-    new_ref,
-    ncx_ref,
-    ncbc_ref,
-    hist_x,
-    hist_bc,
-    own_bc,
-    other_bc,
-    sq_own,
-    sq_other,
-    taps,
-    *rest,
-):
-    bufs = rest[:CHUNKS]
-    t_send, t_recv, x_send, x_recv, p_send, p_recv = rest[CHUNKS:]
+def kernel(n_dp, *refs):
+    operands = refs[:16]
+    y_ref, new_ref, ncx_ref, ncbc_ref = refs[16:20]
+    held_refs = refs[20:36]
+    hist_x, hist_bc, own_bc, other_bc, sq_own, sq_other, xs_rows, b_rows = refs[36:44]
+    bufs = refs[44 : 44 + MESSAGES]
+    in_sem, t_send, t_recv, x_send, x_recv, p_send, p_recv = refs[44 + MESSAGES :]
+    (
+        x_ref,
+        bc_ref,
+        gate_ref,
+        dt_ref,
+        hx_ref,
+        hbc_ref,
+        ssm_ref,
+        wx_ref,
+        wbc_ref,
+        bias_ref,
+        rate_ref,
+        skip_ref,
+        gain_ref,
+        par_ref,
+        acc_ref,
+        dst_ref,
+    ) = held_refs
+    loads = [
+        pltpu.make_async_copy(operands[i], held_refs[i], in_sem.at[i]) for i in range(16)
+    ]
+    names = ("x", "bc", "gate", "dt", "hx", "hbc", "ssm", "wx", "wbc")
+    names += ("bias", "rate", "skip", "gain", "par", "acc", "dst")
+    load = dict(zip(names, loads))
     chips = n_dp // 2
     me = lax.axis_index("dp")
     chip = me // 2
@@ -89,11 +90,17 @@
     for j in range(1, chips):
         pl.semaphore_signal(barrier, inc=1, device_id={"dp": ahead(j)}, device_id_type=MESH)
 
+    order = ("dst", "ssm", "par", "bc", "hbc", "wbc", "acc", "x", "hx", "wx")
+    order += ("dt", "bias", "rate", "gate", "skip", "gain")
+    for name in order:
+        load[name].start()
+
     requests = par_ref.shape[0]
     rows = x_ref.shape[0]
-    heads = dt_ref.shape[1]
+    heads = dt_ref.shape[0]
     width = x_ref.shape[1]
 
+    load["dst"].wait()
     stay = [jnp.int32(0)] * (requests - MOVE)
     move = [jnp.int32(0)] * MOVE
     stay_count = jnp.int32(0)
@@ -106,18 +113,55 @@
             move[k] = jnp.where(jnp.logical_not(staying) & (move_count == k), q, move[k])
         stay_count = stay_count + jnp.where(staying, 1, 0)
         move_count = move_count + jnp.where(staying, 0, 1)
-    source = [jnp.int32(-1)] * IN_CAP
-    arrived = jnp.int32(0)
-    for d in range(n_dp):
-        rank = jnp.int32(0)
-        for q in range(requests):
-            to = dst_ref[d * requests + q]
-            mine = to == me
-            for k in range(IN_CAP):
-                source[k] = jnp.where(mine & (arrived == k), d * MOVE + rank, source[k])
-            arrived = arrived + jnp.where(mine, 1, 0)
-            rank = rank + jnp.where(to >= 0, 1, 0)
-
+    stays = requests - MOVE
+    per = heads // CHUNKS
+    depth_rows = per * P_SIZE
+
+    def block_of(c, device):
+        if c in (TAPS, SCALE):
+            return bufs[c].at[device]
+        return bufs[c].at[pl.ds(device * MOVE, MOVE)]
+
+    def across(c, j, device):
+        return pltpu.make_async_remote_copy(
+            src_ref=block_of(c, device),
+            dst_ref=block_of(c, device),
+            send_sem=x_send.at[c, j],
+            recv_sem=x_recv.at[c, j],
+            device_id={"dp": ahead(j)},
+            device_id_type=MESH,
+        )
+
+    def beside(c, j, device):
+        return pltpu.make_async_remote_copy(
+            src_ref=block_of(c, device),
+            dst_ref=block_of(c, device),
+            send_sem=p_send.at[c, j],
+            recv_sem=p_recv.at[c, j],
+            device_id={"dp": twin},
+            device_id_type=MESH,
+        )
+
+    def send(c):
+        for j in range(1, chips):
+            across(c, j, me).start()
+        beside(c, 0, me).start()
+
+    def relay(c):
+        for j in range(1, chips):
+            across(c, j, behind(j, core)).wait_recv()
+            beside(c, j, behind(j, core)).start()
+
+    load["ssm"].wait()
+    for c in range(RAW):
+        for k in range(MOVE):
+            part = ssm_ref[move[k], c * per : (c + 1) * per]
+            bufs[c][me * MOVE + k] = part.reshape(depth_rows, N)
+    pl.semaphore_wait(barrier, 1 + chips)
+    for c in range(RAW):
+        send(c)
+
+    load["par"].wait()
     row = iota((rows, rows), 0)
     col = iota((rows, rows), 1)
     tile = (iota((NODES, rows), 1) % NODES == iota((NODES, rows), 0)).astype(F32)
@@ -142,19 +186,19 @@
     path = path + mm(hop16, path)
     depth = jnp.sum(path, axis=1, keepdims=True) - 1.0
     hops = [eye, hop1, hop2, hop3]
-    hist_rows = 8 * requests
+    hist_rows = 32
     hist_row = iota((rows, hist_rows), 1)
-    hist_mine = (hist_row // 8 == iota((rows, hist_rows), 0) // NODES) & (hist_row % 8 < 3)
+    hist_mine = (hist_row % 8 == iota((rows, hist_rows), 0) // NODES) & (hist_row < 24)
     lags = [
-        jnp.where(hist_mine & ((hist_row % 8).astype(F32) == 3.0 - k + depth), 1.0, 0.0)
+        jnp.where(hist_mine & ((hist_row // 8).astype(F32) == 3.0 - k + depth), 1.0, 0.0)
         for k in range(4)
     ]
 
     hist_x[...] = jnp.zeros(hist_x.shape, F32)
     hist_bc[...] = jnp.zeros(hist_bc.shape, F32)
-    for r in range(requests):
-        hist_x[8 * r : 8 * r + 3, :] = hx_ref[r].astype(F32)
-        hist_bc[8 * r : 8 * r + 3, :] = hbc_ref[r].astype(F32)
+    load["hbc"].wait()
+    for t in range(3):
+        hist_bc[8 * t : 8 * t + requests, :] = hbc_ref[t].astype(F32)
 
     def convolve(values, history, w_ref):
         summed = w_ref[0:1, :].astype(F32) * values.astype(F32)
@@ -163,9 +207,10 @@
             summed = summed + w_ref[k : k + 1, :].astype(F32) * tap
         return silu(summed).astype(BF16)
 
+    load["bc"].wait()
+    load["wbc"].wait()
     own_bc[...] = convolve(bc_ref[...], hist_bc[...], wbc_ref)
 
-    pl.semaphore_wait(barrier, 1 + chips)
     bc_copy = pltpu.make_async_remote_copy(
         src_ref=own_bc,
         dst_ref=other_bc,
@@ -176,12 +221,34 @@
     )
     bc_copy.start()
 
+    source = [jnp.int32(-1)] * IN_CAP
+    arrived = jnp.int32(0)
+    for d in range(n_dp):
+        rank = jnp.int32(0)
+        for q in range(requests):
+            to = dst_ref[d * requests + q]
+            mine = to == me
+            for k in range(IN_CAP):
+                source[k] = jnp.where(mine & (arrived == k), d * MOVE + rank, source[k])
+            arrived = arrived + jnp.where(mine, 1, 0)
+            rank = rank + jnp.where(to >= 0, 1, 0)
+
+    load["acc"].wait()
+    for name in ("hx", "x", "wx", "dt", "bias", "rate"):
+        load[name].wait()
+    for t in range(3):
+        hist_x[8 * t : 8 * t + requests, :] = hx_ref[t].astype(F32)
     x_act = convolve(x_ref[...], hist_x[...], wx_ref)
 
-    raw = dt_ref[...].astype(F32) + bias_ref[...]
-    step = jnp.maximum(raw, 0.0) + jnp.log1p(jnp.exp(-jnp.abs(raw)))
-    step_decay = -rate_ref[...] * step
-    log = mm_exact(path, step_decay)
+    head_eye = iota((heads, heads), 0) == iota((heads, heads), 1)
+
+    def head_column(ref):
+        return jnp.sum(jnp.where(head_eye, ref[...], 0.0), axis=1, keepdims=True)
+
+    raw = dt_ref[...].astype(F32) + head_column(bias_ref)
+    step_t = jnp.maximum(raw, 0.0) + jnp.log1p(jnp.exp(-jnp.abs(raw)))
+    step = step_t.T
+    log = mm_exact(path, (-head_column(rate_ref) * step_t).T)
 
     target = jnp.zeros((rows, rows), jnp.int32)
     for r in range(requests):
@@ -205,7 +272,9 @@
         )
 
     x_float = x_act.astype(F32)
-    scaled_t = (expand(coef) * x_float).T.astype(BF16)
+    scaled = expand(coef) * x_float
+    scaled_t = scaled.T.astype(BF16)
+    xs_rows[...] = scaled.astype(BF16).reshape(xs_rows.shape)
 
     def tap_rows():
         pick = iota((8 * requests, rows), 0)
@@ -227,12 +296,12 @@
         return fx.astype(BF16), fbc.astype(BF16)
 
     fresh_x, fresh_bc = tap_rows()
-    stays = requests - MOVE
-    taps[me] = jnp.concatenate([fresh_x[8 * stays :], fresh_bc[8 * stays :]], axis=1)
+    bufs[TAPS][me] = jnp.concatenate([fresh_x[8 * stays :], fresh_bc[8 * stays :]], axis=1)
     for k in range(stays):
         ncx_ref[k] = fresh_x[8 * k : 8 * k + 3]
         ncbc_ref[k] = fresh_bc[8 * k : 8 * k + 3]
 
+    send(TAPS)
     bc_copy.wait()
     own = own_bc[...]
     other = other_bc[...]
@@ -244,14 +313,16 @@
 
     row_request = iota((rows, 1), 0) // NODES
     first_row = iota((rows, 1), 0)
-    per = heads // CHUNKS
-    depth_rows = per * P_SIZE
+    b_rows[...] = b_act.reshape(b_rows.shape)
+
+    def scale_of(request):
+        return jnp.sum(
+            jnp.where(first_row == NODES * request, accept_exp, 0.0), axis=0, keepdims=True
+        )
 
     def fresh_of(request):
         b_mine = jnp.where(row_request == request, b_act.astype(F32), 0.0).astype(BF16)
-        scale = jnp.sum(
-            jnp.where(first_row == NODES * request, accept_exp, 0.0), axis=0, keepdims=True
-        )
+        scale = scale_of(request)
 
         def chunk(c):
             update = mm(scaled_t[c * depth_rows : (c + 1) * depth_rows], b_mine)
@@ -264,49 +335,14 @@
 
         return chunk
 
-    def block_of(c, device):
-        if c == CHUNKS:
-            return taps.at[device]
-        return bufs[c].at[pl.ds(device * MOVE, MOVE)]
-
-    def across(c, j, device):
-        return pltpu.make_async_remote_copy(
-            src_ref=block_of(c, device),
-            dst_ref=block_of(c, device),
-            send_sem=x_send.at[c, j],
-            recv_sem=x_recv.at[c, j],
-            device_id={"dp": ahead(j)},
-            device_id_type=MESH,
-        )
-
-    def beside(c, j, device):
-        return pltpu.make_async_remote_copy(
-            src_ref=block_of(c, device),
-            dst_ref=block_of(c, device),
-            send_sem=p_send.at[c, j],
-            recv_sem=p_recv.at[c, j],
-            device_id={"dp": twin},
-            device_id_type=MESH,
-        )
-
-    def send(c):
-        for j in range(1, chips):
-            across(c, j, me).start()
-        beside(c, 0, me).start()
-
-    def relay(c):
-        for j in range(1, chips):
-            across(c, j, behind(j, core)).wait_recv()
-            beside(c, j, behind(j, core)).start()
-
     def place(c):
         for j in range(chips):
             beside(c, j, behind(j, 1 - core)).wait_recv()
         for k in range(IN_CAP):
             index = jnp.maximum(source[k], 0)
             there = source[k] >= 0
-            if c == CHUNKS:
-                found = taps[index // MOVE].astype(F32)
+            if c == TAPS:
+                found = bufs[TAPS][index // MOVE].astype(F32)
                 found = jnp.where(index % MOVE == 0, found[0:8], found[8:16])
                 found = jnp.where(there, found, 0.0).astype(BF16)
                 ncx_ref[stays + k] = found[0:3, :width]
@@ -315,20 +351,52 @@
                 found = jnp.where(there, bufs[c][index].astype(F32), 0.0).astype(BF16)
                 new_ref[stays + k, c * per : (c + 1) * per] = found.reshape(per, P_SIZE, N)
 
+    raw_width = RAW * depth_rows
+    bufs[SCALE][me] = jnp.zeros(bufs[SCALE].shape[1:], F32)
+    for k in range(MOVE):
+        bufs[SCALE][me, k : k + 1, :heads] = scale_of(move[k])
+        bufs[AUX][me * MOVE + k, :, :raw_width] = xs_rows[move[k]][:, :raw_width]
+        bufs[AUX][me * MOVE + k, :, raw_width:] = b_rows[move[k]]
+    send(SCALE)
+    send(AUX)
+
+    def settle(messages):
+        for c in messages:
+            for j in range(chips):
+                beside(c, j, behind(j, 1 - core)).wait_recv()
+
+    def place_raw():
+        settle((SCALE, AUX) + tuple(range(RAW)))
+        for k in range(IN_CAP):
+            index = jnp.maximum(source[k], 0)
+            there = source[k] >= 0
+            scales = bufs[SCALE][index // MOVE]
+            scale = jnp.where(index % MOVE == 0, scales[0:1], scales[1:2])
+            both = bufs[AUX][index].astype(F32)
+            update = mm(both[:, :raw_width].T, both[:, raw_width:])
+            for head in range(RAW * per):
+                low = (head % per) * P_SIZE
+                held = bufs[head // per][index][low : low + P_SIZE].astype(F32)
+                found = held * scale[:, head : head + 1]
+                found = found + update[head * P_SIZE : (head + 1) * P_SIZE]
+                new_ref[stays + k, head] = jnp.where(there, found, 0.0).astype(BF16)
+
     movers = [fresh_of(move[k]) for k in range(MOVE)]
-    for c in range(CHUNKS):
+    for c in range(RAW, CHUNKS):
         for k in range(MOVE):
             bufs[c][me * MOVE + k] = movers[k](c)
         send(c)
-    send(CHUNKS)
-
+    for c in range(RAW):
+        relay(c)
+
+    for name in ("gate", "skip", "gain"):
+        load[name].wait()
     inner = lax.dot_general(
         c_act, b_act, (((1,), (1,)), ((), ())), preferred_element_type=F32
     )
     inside = path > 0.5
     inner = jnp.where(inside, inner, 0.0)
     log_t = log.T
-    step_t = step.T
     log_exp = expand(jnp.exp(log))
     held = jnp.concatenate(
         [
@@ -368,7 +436,9 @@
     )
     sq_copy.start()
 
-    relay(0)
+    relay(TAPS)
+    relay(SCALE)
+    relay(AUX)
     for k in range(stays):
         chunk = fresh_of(stay[k])
         for c in range(CHUNKS):
@@ -379,15 +449,26 @@
     mean_square = (squares + partner) * (1.0 / (2 * heads * P_SIZE))
     y_ref[...] = (gated * lax.rsqrt(mean_square + 1e-05) * gain_ref[...]).astype(BF16)
 
-    for c in range(1, CHUNKS + 1):
+    relay(RAW)
+    place_raw()
+    place(TAPS)
+    for c in range(RAW + 1, CHUNKS):
         relay(c)
         place(c - 1)
-    place(CHUNKS)
-    for c in range(CHUNKS + 1):
+    place(CHUNKS - 1)
+    for c in range(MESSAGES):
         for j in range(1, chips):
             across(c, j, me).wait_send()
         for j in range(chips):
             beside(c, j, behind(j, core)).wait_send()
+
+
+def write_out(*refs):
+    copies = [pltpu.make_async_copy(refs[i], refs[4 + i], refs[8].at[i]) for i in range(4)]
+    for copy in copies:
+        copy.start()
+    for copy in copies:
+        copy.wait()
 
 
 def body(
@@ -414,44 +495,13 @@
     bc_width = bc_stream.shape[1]
     requests = parents.shape[0]
     heads = dt_stream.shape[1]
-    vmem = pl.BlockSpec(memory_space=pltpu.VMEM)
-    smem = pl.BlockSpec(memory_space=pltpu.SMEM)
-    copies = (CHUNKS + 1, chips)
-    return pl.pallas_call(
-        functools.partial(kernel, n_dp),
-        out_shape=(
-            jax.ShapeDtypeStruct((rows, width), BF16),
-            jax.ShapeDtypeStruct((KEEP, heads, P_SIZE, N), BF16),
-            jax.ShapeDtypeStruct((KEEP, 3, width), BF16),
-            jax.ShapeDtypeStruct((KEEP, 3, bc_width), BF16),
-        ),
-        in_specs=[vmem] * 14 + [smem] * 2,
-        out_specs=(vmem,) * 4,
-        scratch_shapes=[
-            pltpu.VMEM((8 * requests, width), F32),
-            pltpu.VMEM((8 * requests, bc_width), F32),
-            pltpu.VMEM((rows, bc_width), BF16),
-            pltpu.VMEM((rows, bc_width), BF16),
-            pltpu.VMEM((8, rows), F32),
-            pltpu.VMEM((8, rows), F32),
-            pltpu.VMEM((n_dp, 8 * MOVE, width + bc_width), BF16),
-        ]
-        + [
-            pltpu.VMEM((n_dp * MOVE, heads // CHUNKS * P_SIZE, N), BF16) for _ in range(CHUNKS)
-        ]
-        + [pltpu.SemaphoreType.DMA((2,))] * 2
-        + [pltpu.SemaphoreType.DMA(copies)] * 4,
-        compiler_params=pltpu.CompilerParams(
-            collective_id=0, has_side_effects=True, vmem_limit_bytes=40 << 20
-        ),
-        name="verify_and_migrate",
-    )(
+    operands = (
         x_stream,
         bc_stream,
         gate_stream,
-        dt_stream,
-        conv_x_state,
-        conv_bc_state,
+        dt_stream.T,
+        conv_x_state.transpose(1, 0, 2),
+        conv_bc_state.transpose(1, 0, 2),
         ssm_state,
         conv_x_weight,
         conv_bc_weight,
@@ -463,6 +513,58 @@
         accepted,
         destination,
     )
+    vmem = pl.BlockSpec(memory_space=pltpu.VMEM)
+    hbm = pl.BlockSpec(memory_space=pltpu.HBM)
+    outs = (
+        jax.ShapeDtypeStruct((rows, width), BF16),
+        jax.ShapeDtypeStruct((KEEP, heads, P_SIZE, N), BF16),
+        jax.ShapeDtypeStruct((KEEP, 3, width), BF16),
+        jax.ShapeDtypeStruct((KEEP, 3, bc_width), BF16),
+    )
+    copies = (MESSAGES, chips)
+    part = heads // CHUNKS * P_SIZE
+    results = pl.pallas_call(
+        functools.partial(kernel, n_dp),
+        out_shape=outs,
+        in_specs=[hbm] * 16,
+        out_specs=(vmem,) * 4,
+        scratch_shapes=[
+            (pltpu.VMEM if i < 14 else pltpu.SMEM)(a.shape, a.dtype)
+            for i, a in enumerate(operands)
+        ]
+        + [
+            pltpu.VMEM((32, width), F32),
+            pltpu.VMEM((32, bc_width), F32),
+            pltpu.VMEM((rows, bc_width), BF16),
+            pltpu.VMEM((rows, bc_width), BF16),
+            pltpu.VMEM((8, rows), F32),
+            pltpu.VMEM((8, rows), F32),
+            pltpu.VMEM((requests, NODES, width), BF16),
+            pltpu.VMEM((requests, NODES, bc_width), BF16),
+        ]
+        + [pltpu.VMEM((n_dp * MOVE, part, N), BF16)] * CHUNKS
+        + [
+            pltpu.VMEM((n_dp, 8 * MOVE, width + bc_width), BF16),
+            pltpu.VMEM((n_dp * MOVE, NODES, RAW * part + bc_width), BF16),
+            pltpu.VMEM((n_dp, 8, 128), F32),
+        ]
+        + [pltpu.SemaphoreType.DMA((16,))]
+        + [pltpu.SemaphoreType.DMA((2,))] * 2
+        + [pltpu.SemaphoreType.DMA(copies)] * 4,
+        compiler_params=pltpu.CompilerParams(
+            collective_id=0, has_side_effects=True, vmem_limit_bytes=40 << 20
+        ),
+        name="verify_and_migrate",
+    )(*[pltpu.with_memory_space_constraint(a, pltpu.HBM) for a in operands])
+    return pl.pallas_call(
+        write_out,
+        out_shape=outs,
+        in_specs=[vmem] * 4,
+        out_specs=(hbm,) * 4,
+        scratch_shapes=[pltpu.SemaphoreType.DMA((4,))],
+        compiler_params=pltpu.CompilerParams(vmem_limit_bytes=16 << 20),
+        name="write_out",
+    )(*results)
 
 
 def solution(mesh):

time: 38 us -> 22.1 us (0.58)
  local copies, waits for them, and re-layouts: 15.1 us -> 0 us
  Pallas kernels: 21.8 us -> 21.3 us
    unnamed x33 -> x0, local copies, waits for them, and re-layouts: 15.1 us -> none
    pallas_call x1 -> x2, Pallas kernels: 21.8 us -> 21.3 us  [the longest x1 20.1 us: body(): pl.pallas_call(functools.partial(kernel, n_dp), out_shape=outs, in_specs=...]
where the time goes in v2:
time: 22.1 us; the launch traced here: 22 us
  Pallas kernels  21.3 us (96%)
  between operations  0.65 us (3%)
    pallas_call x1, Pallas kernels, body(): pl.pallas_call(functools.partial(kernel, n_dp), out_shape=outs, in_specs=...  20.1 us
    pallas_call x1, Pallas kernels, body(): pl.pallas_call(write_out, out_shape=outs, in_specs=[vmem] * 4, out_specs=...  1.23 us

profile of v2, /device:TPU:0, one launch (start us, length us, event | category | flops | bytes accessed | tf_op | source)
XLA Modules:
  0.0 22.0 jit_solution(2965876098722063538)
XLA Ops:
  0.6 20.1 %verify_and_migrate.1 = (bf16[128,512]{1,0:T(8,128)(2,1)S(1)}, bf16[6,8,64,256]{3,2,1,0:T(8,128)(2,1)S(1)}, bf16[6,3,512]{2,1,0:T(4,128)(2,1)S(1)}, bf16[6,3,256]{2,1,0:T(4,128)(2,1)S(1)}) custom-call(bf16[128,512]{1,0:T(8,128)(2,1)} %refs_0_.1, bf16[128,256]{1,0:T(8,128)(2,1)} %refs_1_.1, bf16[128,512]{1,0:T(8,128)(2,1)} %refs_2_.1, ...), custom_call_target="tpu_custom_call" | custom-call | tf_op jit(solution)/shard_map/verify_and_migrate/pallas_call | solution.py:526
  20.7 1.2 %write_out.1 = (bf16[128,512]{1,0:T(8,128)(2,1)}, bf16[6,8,64,256]{3,2,1,0:T(8,128)(2,1)}, bf16[6,3,512]{2,1,0:T(4,128)(2,1)}, bf16[6,3,256]{2,1,0:T(4,128)(2,1)}) custom-call(bf16[128,512]{1,0:T(8,128)(2,1)S(1)} %get-tuple-element.8.refs_0_, bf16[6,8,64,256]{3,2,1,0:T(8,128)(2,1)S(1)} %get-tuple-element.9.refs_1_, ...), custom_call_target="tpu_custom_call" | custom-call | tf_op jit(solution)/shard_map/write_out/pallas_call | solution.py:559

commit v3 on v2

--- a/solution.py
+++ b/solution.py
@@ -13,8 +13,8 @@
 MOVE = 2
 IN_CAP = 4
 KEEP = 6
-CHUNKS = 8
-RAW = 4
+CHUNKS = 4
+RAW = 2
 TAPS, AUX, SCALE = CHUNKS, CHUNKS + 1, CHUNKS + 2
 MESSAGES = CHUNKS + 3
 MESH = pl.DeviceIdType.MESH
@@ -303,6 +303,8 @@
 
     send(TAPS)
     bc_copy.wait()
+    for c in range(RAW):
+        relay(c)
     own = own_bc[...]
     other = other_bc[...]
     even = (parity == 0).astype(F32)
@@ -386,9 +388,6 @@
         for k in range(MOVE):
             bufs[c][me * MOVE + k] = movers[k](c)
         send(c)
-    for c in range(RAW):
-        relay(c)
-
     for name in ("gate", "skip", "gain"):
         load[name].wait()
     inner = lax.dot_general(

time: 22.1 us -> 21.9 us (level)
  no operation moved by 1% of the time
where the time goes in v3:
time: 21.9 us; the launch traced here: 21.8 us
  Pallas kernels  21.1 us (96%)
  between operations  0.65 us (3%)
    pallas_call x1, Pallas kernels, body(): pl.pallas_call(functools.partial(kernel, n_dp), out_shape=outs, in_specs=...  19.9 us
    pallas_call x1, Pallas kernels, body(): pl.pallas_call(write_out, out_shape=outs, in_specs=[vmem] * 4, out_specs=...  1.23 us

profile of v3, /device:TPU:0, one launch (start us, length us, event | category | flops | bytes accessed | tf_op | source)
XLA Modules:
  0.0 21.8 jit_solution(13635741032811475691)
XLA Ops:
  0.6 19.9 %verify_and_migrate.1 = (bf16[128,512]{1,0:T(8,128)(2,1)S(1)}, bf16[6,8,64,256]{3,2,1,0:T(8,128)(2,1)S(1)}, bf16[6,3,512]{2,1,0:T(4,128)(2,1)S(1)}, bf16[6,3,256]{2,1,0:T(4,128)(2,1)S(1)}) custom-call(bf16[128,512]{1,0:T(8,128)(2,1)} %refs_0_.1, bf16[128,256]{1,0:T(8,128)(2,1)} %refs_1_.1, bf16[128,512]{1,0:T(8,128)(2,1)} %refs_2_.1, ...), custom_call_target="tpu_custom_call" | custom-call | tf_op jit(solution)/shard_map/verify_and_migrate/pallas_call | solution.py:525
  20.5 1.2 %write_out.1 = (bf16[128,512]{1,0:T(8,128)(2,1)}, bf16[6,8,64,256]{3,2,1,0:T(8,128)(2,1)}, bf16[6,3,512]{2,1,0:T(4,128)(2,1)}, bf16[6,3,256]{2,1,0:T(4,128)(2,1)}) custom-call(bf16[128,512]{1,0:T(8,128)(2,1)S(1)} %get-tuple-element.8.refs_0_, bf16[6,8,64,256]{3,2,1,0:T(8,128)(2,1)S(1)} %get-tuple-element.9.refs_1_, ...), custom_call_target="tpu_custom_call" | custom-call | tf_op jit(solution)/shard_map/write_out/pallas_call | solution.py:558
